TPU v7x, 128 devices: a whole 4x4x4 slice. The times are simulated.
128 devices in a mesh: river: 8 (over y, core), coast: 16 (over z, x).
Axes of the slice: x: 4, y: 4, z: 4, core: 2. Of those that a mesh axis runs over, the one named last changes fastest.
Arguments:
- reach_depth: float32 [8192, 128], P(('river', 'coast')), may hold values from 0.02 to 4
- reach_flow: float32 [8192, 128], P(('river', 'coast')), may hold values from -3 to 3
- reach_bed: float32 [8192, 128], P(('river', 'coast')), may hold values from 0 to 1
- reach_width: float32 [8192, 128], P(('river', 'coast')), may hold values from 200 to 800
- reach_length: float32 [8192, 128], P(('river', 'coast')), may hold values from 4000 to 12000
- runoff: float32 [8192, 128], P(('river', 'coast')), may hold values from 1 to 100
- flows_into: int32 [8192, 128], P(('river', 'coast')), may hold values from 1 to 128, as said below
- mouth_prev: float32 [8192, 32], P(('river', 'coast')), may hold values from -1.5 to 1.5
- mouth_tile: int32 [8192, 32, 1], P(('river', 'coast')), may hold values from 0 to 127; in each aligned block of 2048 rows (0 to 2047, 2048 to 4095, ..., all dimensions but the last counted through in order) at most 32 rows name the same one
- mouth_cell: int32 [8192, 32], P(('river', 'coast')), may hold values from 0 to 4095
- sea_level: float32 [256, 2048], P('river', 'coast'), may hold values from -1.2 to 1.2
- sea_bed: float32 [256, 2048], P('river', 'coast'), may hold values from -4 to 0.5
- wet_mask: int32 [256, 2048], P('river', 'coast'), may hold values 0 or 1
- flux_east: float32 [256, 2048], P('river', 'coast'), may hold values from -3 to 3
- flux_north: float32 [256, 2048], P('river', 'coast'), may hold values from -3 to 3
Outputs:
- depth_after: float32 [8192, 128], P(('river', 'coast'))
- level_after: float32 [256, 2048], P('river', 'coast')
- mouth_level: float32 [8192, 384], P(('river', 'coast'))
Inputs may be any that keep to these rules, and one draw needn't show every extreme that they name: `flows_into`: in every block the last 32 reaches have the value 128 (they flow to the sea); every other reach i names a reach of the same block with index i + 1 to i + 16. `mouth_tile`: among the mouths of one device (the rows of one device, in order), no tile is named more than 32 times, a bound that some block reaches; every tile is named by some mouth.
All inputs are finite; a program needn't handle non-finite values. No bound on the sum of `wet_mask` on one device may be relied on, other than what follows from the above.
Results may differ from a plain program's by a relative error of at most 0.0002.
Values sent between devices are 32-bit elements; how exact they have to be, the bound alone decides.
A program may use at most 64 MiB of HBM per device.

v0:
```python
import jax
import jax.numpy as jnp
from jax import lax
from jax.sharding import PartitionSpec as P

RB = 128
MPB = 32
STEPS = 12


gravity = 9.81
step_seconds = 300.0
cell_metres = 3000.0
river_manning = 0.035
ocean_manning = 0.025
depth_floor = 0.05
reach_offsets = 16


def padded_2(shard, sides, width):
    for axis, dim in sides:
        size, length = (lax.axis_size(axis), shard.shape[dim])
        up = [(i, (i + 1) % size) for i in range(size - 1)]
        down = [(j, i) for i, j in up]
        last = lax.slice_in_dim(shard, length - width, length, axis=dim)
        leading = lax.slice_in_dim(shard, 0, width, axis=dim)
        before = lax.ppermute(last, axis, up)
        after = lax.ppermute(leading, axis, down)
        shard = jnp.concatenate([before, shard, after], axis=dim)
    return shard


def from_behind(block, axis, distance):
    devices = range(lax.axis_size(axis))
    route = [(i - distance, i) for i in devices if i - distance in devices]
    return lax.ppermute(block, axis, route)


def inertial(unit_flow, upper_level, lower_level, bed_upper, bed_lower, distance, manning):
    face_depth = jnp.maximum(upper_level, lower_level) - jnp.maximum(bed_upper, bed_lower)
    driving = (
        gravity
        * step_seconds
        * jnp.maximum(face_depth, 0.0)
        * (upper_level - lower_level)
        / distance
    )
    friction = (
        gravity
        * step_seconds
        * manning
        * manning
        * jnp.abs(unit_flow)
        / jnp.power(jnp.maximum(face_depth, depth_floor), 7.0 / 3.0)
    )
    return (unit_flow + driving) / (1.0 + friction)


def look_down(values, offset_masks):
    blocks = values.shape[0]
    inland = offset_masks[0].shape[1]
    padded = jnp.concatenate([values, jnp.zeros((blocks, reach_offsets), jnp.float32)], axis=1)
    found = jnp.zeros((blocks, inland), jnp.float32)
    for offset in range(1, reach_offsets + 1):
        found = found + jnp.where(
            offset_masks[offset - 1], padded[:, offset : offset + inland], 0.0
        )
    return found


def gather_inflow(discharge_inland, offset_masks):
    blocks, inland = discharge_inland.shape
    total = jnp.zeros((blocks, RB + reach_offsets), jnp.float32)
    for offset in range(1, reach_offsets + 1):
        moved = jnp.where(offset_masks[offset - 1], discharge_inland, 0.0)
        placed = jnp.concatenate(
            [
                jnp.zeros((blocks, offset), jnp.float32),
                moved,
                jnp.zeros((blocks, RB + reach_offsets - offset - inland), jnp.float32),
            ],
            axis=1,
        )
        total = total + placed
    return total[:, :RB]


def river_step(
    water_depth,
    unit_flow,
    reach_bed,
    reach_width,
    reach_length,
    runoff,
    offset_masks,
    bed_down,
    mouth_prev,
):
    inland = RB - MPB
    surface = reach_bed + water_depth
    below = jnp.concatenate([look_down(surface, offset_masks), mouth_prev], axis=1)
    unit_flow = inertial(
        unit_flow, surface, below, reach_bed, bed_down, reach_length, river_manning
    )
    discharge = unit_flow * reach_width
    inflow = gather_inflow(discharge[:, :inland], offset_masks)
    water_depth = water_depth + step_seconds * (inflow + runoff - discharge) / (
        reach_width * reach_length
    )
    return (water_depth, unit_flow, discharge[:, inland:])


def per_device(
    reach_depth,
    reach_flow,
    reach_bed,
    reach_width,
    reach_length,
    runoff,
    flows_into,
    mouth_prev,
    mouth_tile,
    mouth_cell,
    sea_level,
    sea_bed,
    wet_mask,
    flux_east,
    flux_north,
):
    river_count = lax.axis_size("river")
    coast_count = lax.axis_size("coast")
    devices = river_count * coast_count
    blocks = reach_depth.shape[0]
    tile_rows, tile_cols = sea_level.shape
    mouths = blocks * MPB
    capacity = max(2, 2 * blocks * MPB // devices)
    inland = RB - MPB
    down_index = flows_into[:, :inland]
    position = jnp.arange(inland, dtype=jnp.int32)[None, :]
    offset_masks = [down_index == position + offset for offset in range(1, reach_offsets + 1)]
    bed_down = jnp.concatenate([look_down(reach_bed, offset_masks), reach_bed[:, inland:]], axis=1)
    target = mouth_tile.reshape(mouths)
    sorter = jnp.argsort(target, stable=True)
    sorted_tiles = target[sorter]
    first_index = jnp.searchsorted(sorted_tiles, sorted_tiles, side="left")
    ranked = jnp.arange(mouths, dtype=jnp.int32) - first_index
    slot_index = jnp.zeros((mouths,), jnp.int32).at[sorter].set(ranked)
    cell_index = mouth_cell.reshape(mouths)
    water_level = jnp.where(wet_mask == 1, jnp.maximum(sea_level, sea_bed), sea_bed)
    bed_padded = padded_2(sea_bed, (("river", 0), ("coast", 1)), 1)
    west_row = from_behind(flux_east[tile_rows - 1 :, :], "river", 1)
    south_edge = from_behind(flux_north[:, tile_cols - 1 :], "coast", 1)
    east_faces = jnp.concatenate([west_row, flux_east], axis=0)

    def river_turn(substep, carry):
        water_depth, unit_flow, series = carry
        water_depth, unit_flow, mouth_flow = river_step(
            water_depth,
            unit_flow,
            reach_bed,
            reach_width,
            reach_length,
            runoff,
            offset_masks,
            bed_down,
            mouth_prev,
        )
        series = lax.dynamic_update_slice_in_dim(series, mouth_flow.reshape(1, mouths), substep, 0)
        return (water_depth, unit_flow, series)

    start_series = jnp.zeros((STEPS, mouths), jnp.float32)
    water_depth, unit_flow, series = lax.fori_loop(
        0, STEPS, river_turn, (reach_depth, reach_flow, start_series)
    )
    sending = (
        jnp.zeros((devices, STEPS, capacity), jnp.float32).at[target, :, slot_index].set(series.T)
    )
    labels = jnp.zeros((devices, capacity), jnp.int32).at[target, slot_index].set(cell_index)
    arrived, arrived_cells = (
        lax.all_to_all(
            sending.reshape(devices, STEPS * capacity),
            ("river", "coast"),
            split_axis=0,
            concat_axis=0,
            tiled=True,
        ),
        lax.all_to_all(labels, ("river", "coast"), split_axis=0, concat_axis=0, tiled=True),
    )
    arrived = arrived.reshape(devices, STEPS, capacity)
    flat_cells = arrived_cells.reshape(devices * capacity)
    cell_rows = flat_cells // tile_cols
    cell_cols = flat_cells % tile_cols
    row_hits = (cell_rows[:, None] == jnp.arange(tile_rows, dtype=jnp.int32)[None, :]).astype(
        jnp.float32
    )
    col_hits = (cell_cols[:, None] == jnp.arange(tile_cols, dtype=jnp.int32)[None, :]).astype(
        jnp.float32
    )
    incoming_all = jnp.transpose(arrived, (1, 0, 2)).reshape(STEPS, devices * capacity)
    weighted = incoming_all[:, :, None] * col_hits[None, :, :]
    sources = jnp.einsum("mr,kmc->krc", row_hits, weighted, precision=lax.Precision.HIGHEST)

    def ocean_turn(substep, carry):
        level_now, east_now, north_now, edge_now, replies = carry
        source = lax.dynamic_index_in_dim(sources, substep, 0, keepdims=False)
        padded = padded_2(level_now, (("river", 0), ("coast", 1)), 1)
        east_now = inertial(
            east_now,
            padded[:-1, 1:-1],
            padded[1:, 1:-1],
            bed_padded[:-1, 1:-1],
            bed_padded[1:, 1:-1],
            cell_metres,
            ocean_manning,
        )
        north_now = inertial(
            north_now,
            padded[1:-1, 1:-1],
            padded[1:-1, 2:],
            bed_padded[1:-1, 1:-1],
            bed_padded[1:-1, 2:],
            cell_metres,
            ocean_manning,
        )
        edge_now = inertial(
            edge_now,
            padded[1:-1, 0:1],
            padded[1:-1, 1:2],
            bed_padded[1:-1, 0:1],
            bed_padded[1:-1, 1:2],
            cell_metres,
            ocean_manning,
        )
        north_lower = jnp.concatenate([edge_now, north_now[:, :-1]], axis=1)
        spread = east_now[1:] - east_now[:-1] + north_now - north_lower
        level_now = (
            level_now
            - step_seconds / cell_metres * spread
            + step_seconds / (cell_metres * cell_metres) * source
        )
        picked = level_now.reshape(tile_rows * tile_cols)[flat_cells].reshape(devices, 1, capacity)
        replies = lax.dynamic_update_slice_in_dim(replies, picked, substep, 1)
        return (level_now, east_now, north_now, edge_now, replies)

    start_replies = jnp.zeros((devices, STEPS, capacity), jnp.float32)
    water_level, east_faces, north_faces, south_edge, replies = lax.fori_loop(
        0, STEPS, ocean_turn, (water_level, east_faces, flux_north, south_edge, start_replies)
    )
    returned = lax.all_to_all(
        replies.reshape(devices, STEPS * capacity),
        ("river", "coast"),
        split_axis=0,
        concat_axis=0,
        tiled=True,
    )
    returned = returned.reshape(devices, STEPS, capacity)
    tile_grid = target.reshape(blocks, 1, MPB)
    slot_grid = slot_index.reshape(blocks, 1, MPB)
    step_grid = jnp.arange(STEPS, dtype=jnp.int32).reshape(1, STEPS, 1)
    mouth_level = returned[tile_grid, step_grid, slot_grid].reshape(blocks, STEPS * MPB)
    return (water_depth, water_level, mouth_level)


def solution(mesh):
    placed = (
        P(("river", "coast"), None),
        P(("river", "coast"), None),
        P(("river", "coast"), None),
        P(("river", "coast"), None),
        P(("river", "coast"), None),
        P(("river", "coast"), None),
        P(("river", "coast"), None),
        P(("river", "coast"), None),
        P(("river", "coast"), None, None),
        P(("river", "coast"), None),
        P("river", "coast"),
        P("river", "coast"),
        P("river", "coast"),
        P("river", "coast"),
        P("river", "coast"),
    )
    return jax.shard_map(
        per_device,
        mesh=mesh,
        in_specs=placed,
        out_specs=(P(("river", "coast"), None), P("river", "coast"), P(("river", "coast"), None)),
        check_vma=False,
    )
```

profile of v0, /device:TPU:1, one launch (start us, length us, event | category | flops | bytes accessed | tf_op | source)
XLA Modules:
  0.0 984.1 jit_solution(10586489569613972331)
XLA Ops:
  2.3 5.0 sort.17
  7.4 11.8 %gather_fusion.2 = s32[2048]{0:T(1024)S(1)} fusion(s32[2048]{0:T(1024)S(1)} %reshape.313, s32[2048]{0:T(1024)S(1)} %get-tuple-element.1280), kind=kCustom, calls=%fused_computation.2 | custom fusion | bytes 24576 | tf_op jit(solution)/shard_map/gather | solution.py:144
  19.3 142.4 %while.70 = (s32[]{:T(128)}, u32[2048]{0:T(1024)S(1)}, u32[2048]{0:T(1024)S(1)}, s32[2048]{0:T(1024)S(1)}, s32[]{:T(128)}, /*index=5*/s32[]{:T(128)}, s32[]{}) while((s32[]{:T(128)}, u32[2048]{0:T(1024)S(1)}, u32[2048]{0:T(1024)S(1)}, s32[2048]{0:T(1024)S(1)}, s32[]{:T(128)}, /*index=5*/s32[]{:T(128)}, s32[]{}) %tuple.186), condition=%wide.region_4.5_spmd.clone, body=%wide.region_3.4_spmd.clone.sunk | while | flops 38916 | bytes 135269 | solution.py:145
  19.3 11.8 %gather_fusion.1 = s32[2048]{0:T(1024)S(1)} fusion(s32[2048]{0:T(1024)S(1)} %get-tuple-element.1735, u32[2048]{0:T(1024)S(1)} %broadcast_clamp_fusion.6), kind=kCustom, calls=%fused_computation.clone.clone.1 | custom fusion | bytes 24576 | tf_op jit(solution)/shard_map/jit(searchsorted)/jit(_searchsorted_scan_impl)/vmap(jit(_searchsorted_scan_impl))/while/body/eval_jaxpr/gather | solution.py:145
  31.2 11.8 %gather_fusion.1 = s32[2048]{0:T(1024)S(1)} fusion(s32[2048]{0:T(1024)S(1)} %get-tuple-element.1735, u32[2048]{0:T(1024)S(1)} %broadcast_clamp_fusion.6), kind=kCustom, calls=%fused_computation.clone.clone.1 | custom fusion | bytes 24576 | tf_op jit(solution)/shard_map/jit(searchsorted)/jit(_searchsorted_scan_impl)/vmap(jit(_searchsorted_scan_impl))/while/body/eval_jaxpr/gather | solution.py:145
  43.1 11.8 %gather_fusion.1 = s32[2048]{0:T(1024)S(1)} fusion(s32[2048]{0:T(1024)S(1)} %get-tuple-element.1735, u32[2048]{0:T(1024)S(1)} %broadcast_clamp_fusion.6), kind=kCustom, calls=%fused_computation.clone.clone.1 | custom fusion | bytes 24576 | tf_op jit(solution)/shard_map/jit(searchsorted)/jit(_searchsorted_scan_impl)/vmap(jit(_searchsorted_scan_impl))/while/body/eval_jaxpr/gather | solution.py:145
  55.0 11.8 %gather_fusion.1 = s32[2048]{0:T(1024)S(1)} fusion(s32[2048]{0:T(1024)S(1)} %get-tuple-element.1735, u32[2048]{0:T(1024)S(1)} %broadcast_clamp_fusion.6), kind=kCustom, calls=%fused_computation.clone.clone.1 | custom fusion | bytes 24576 | tf_op jit(solution)/shard_map/jit(searchsorted)/jit(_searchsorted_scan_impl)/vmap(jit(_searchsorted_scan_impl))/while/body/eval_jaxpr/gather | solution.py:145
  66.8 11.8 %gather_fusion.1 = s32[2048]{0:T(1024)S(1)} fusion(s32[2048]{0:T(1024)S(1)} %get-tuple-element.1735, u32[2048]{0:T(1024)S(1)} %broadcast_clamp_fusion.6), kind=kCustom, calls=%fused_computation.clone.clone.1 | custom fusion | bytes 24576 | tf_op jit(solution)/shard_map/jit(searchsorted)/jit(_searchsorted_scan_impl)/vmap(jit(_searchsorted_scan_impl))/while/body/eval_jaxpr/gather | solution.py:145
  78.7 11.8 %gather_fusion.1 = s32[2048]{0:T(1024)S(1)} fusion(s32[2048]{0:T(1024)S(1)} %get-tuple-element.1735, u32[2048]{0:T(1024)S(1)} %broadcast_clamp_fusion.6), kind=kCustom, calls=%fused_computation.clone.clone.1 | custom fusion | bytes 24576 | tf_op jit(solution)/shard_map/jit(searchsorted)/jit(_searchsorted_scan_impl)/vmap(jit(_searchsorted_scan_impl))/while/body/eval_jaxpr/gather | solution.py:145
  90.6 11.8 %gather_fusion.1 = s32[2048]{0:T(1024)S(1)} fusion(s32[2048]{0:T(1024)S(1)} %get-tuple-element.1735, u32[2048]{0:T(1024)S(1)} %broadcast_clamp_fusion.6), kind=kCustom, calls=%fused_computation.clone.clone.1 | custom fusion | bytes 24576 | tf_op jit(solution)/shard_map/jit(searchsorted)/jit(_searchsorted_scan_impl)/vmap(jit(_searchsorted_scan_impl))/while/body/eval_jaxpr/gather | solution.py:145
  102.4 11.8 %gather_fusion.1 = s32[2048]{0:T(1024)S(1)} fusion(s32[2048]{0:T(1024)S(1)} %get-tuple-element.1735, u32[2048]{0:T(1024)S(1)} %broadcast_clamp_fusion.6), kind=kCustom, calls=%fused_computation.clone.clone.1 | custom fusion | bytes 24576 | tf_op jit(solution)/shard_map/jit(searchsorted)/jit(_searchsorted_scan_impl)/vmap(jit(_searchsorted_scan_impl))/while/body/eval_jaxpr/gather | solution.py:145
  114.3 11.8 %gather_fusion.1 = s32[2048]{0:T(1024)S(1)} fusion(s32[2048]{0:T(1024)S(1)} %get-tuple-element.1735, u32[2048]{0:T(1024)S(1)} %broadcast_clamp_fusion.6), kind=kCustom, calls=%fused_computation.clone.clone.1 | custom fusion | bytes 24576 | tf_op jit(solution)/shard_map/jit(searchsorted)/jit(_searchsorted_scan_impl)/vmap(jit(_searchsorted_scan_impl))/while/body/eval_jaxpr/gather | solution.py:145
  126.2 11.8 %gather_fusion.1 = s32[2048]{0:T(1024)S(1)} fusion(s32[2048]{0:T(1024)S(1)} %get-tuple-element.1735, u32[2048]{0:T(1024)S(1)} %broadcast_clamp_fusion.6), kind=kCustom, calls=%fused_computation.clone.clone.1 | custom fusion | bytes 24576 | tf_op jit(solution)/shard_map/jit(searchsorted)/jit(_searchsorted_scan_impl)/vmap(jit(_searchsorted_scan_impl))/while/body/eval_jaxpr/gather | solution.py:145
  138.0 11.8 %gather_fusion.1 = s32[2048]{0:T(1024)S(1)} fusion(s32[2048]{0:T(1024)S(1)} %get-tuple-element.1735, u32[2048]{0:T(1024)S(1)} %broadcast_clamp_fusion.6), kind=kCustom, calls=%fused_computation.clone.clone.1 | custom fusion | bytes 24576 | tf_op jit(solution)/shard_map/jit(searchsorted)/jit(_searchsorted_scan_impl)/vmap(jit(_searchsorted_scan_impl))/while/body/eval_jaxpr/gather | solution.py:145
  149.9 11.8 %gather_fusion.1 = s32[2048]{0:T(1024)S(1)} fusion(s32[2048]{0:T(1024)S(1)} %get-tuple-element.1735, u32[2048]{0:T(1024)S(1)} %broadcast_clamp_fusion.6), kind=kCustom, calls=%fused_computation.clone.clone.1 | custom fusion | bytes 24576 | tf_op jit(solution)/shard_map/jit(searchsorted)/jit(_searchsorted_scan_impl)/vmap(jit(_searchsorted_scan_impl))/while/body/eval_jaxpr/gather | solution.py:145
  161.7 8.0 scatter_custom_fusion
  170.2 8.1 scatter_custom_fusion.2
  179.0 11.5 %all-to-all-start.1 = ((s32[128,1,32]{2,1,0:T(1,128)}), s32[128,1,32]{2,1,0:T(1,128)S(1)}, u32[]{:S(2)}, u32[]{:S(2)}) async-start(s32[128,1,32]{2,1,0:T(1,128)} %copy.50), calls=%async_computation.1 | async-start | bytes 131072 | tf_op jit(solution)/shard_map/all_to_all | solution.py:187
  205.5 33.0 %while.68 = (s32[]{:T(128)}, f32[64,128]{1,0:T(8,128)S(1)}, f32[64,128]{1,0:T(8,128)S(1)}, f32[12,2048]{1,0:T(8,128)S(1)}, f32[64,128]{1,0:T(8,128)S(1)}, /*inde...) while((s32[]{:T(128)}, f32[64,128]{1,0:T(8,128)S(1)}, ...), condition=%wide.region_1.2_spmd, body=%wide.region_0.1_spmd.sunk | while | flops 886786 | bytes 2274661 | solution.py:172
  239.6 6.2 scatter_custom_fusion.1
  255.5 10.9 %all-to-all-start = ((f32[128,1,384]{2,1,0:T(1,128)}), f32[128,1,384]{2,1,0:T(1,128)S(1)}, u32[]{:S(2)}, u32[]{:S(2)}) async-start(f32[128,1,384]{2,1,0:T(1,128)} %copy.46), calls=%async_computation | async-start | bytes 393216 | tf_op jit(solution)/shard_map/all_to_all | solution.py:180
  270.7 6.4 all-to-all-done
  278.0 12.3 %fusion.47 = f32[12,32,128]{2,1,0:T(8,128)S(1)} fusion(f32[4096,128]{1,0:T(8,128)} %fusion.46, f32[12,4096]{1,0:T(8,128)S(1)} %mul.199, s32[4096]{0:T(1024)S(1)} %get-tuple-element.1274), kind=kOutput, calls=%fused_computation.124 | convolution fusion | flops 2422341632 | bytes 2506752 | tf_op jit(solution)/shard_map/mr,kmc->krc/dot_general | solution.py:201
  290.2 466.1 %while.69 = (s32[]{:T(128)}, f32[32,128]{1,0:T(8,128)S(1)}, f32[33,128]{1,0:T(8,128)S(1)}, f32[32,128]{1,0:T(8,128)S(1)}, f32[32,1]{1,0:T(8,128)S(1)}, /*index=5...) while((s32[]{:T(128)}, f32[32,128]{1,0:T(8,128)S(1)}, ...), condition=%wide.region_9.10_spmd, body=%wide.region_8.9_spmd.sunk | while | flops 191297 | bytes 539809 | solution.py:246
  302.9 23.0 %gather_fusion = f32[4096]{0:T(1024)S(1)} fusion(f32[4096]{0:T(1024)S(1)} %bitcast.48, s32[4096]{0:T(1024)S(1)} %broadcast_clamp_fusion.5), kind=kCustom, calls=%fused_computation.1.clone.1 | custom fusion | bytes 49152 | tf_op jit(solution)/shard_map/while/body/eval_jaxpr/gather | solution.py:241
  341.0 23.0 %gather_fusion = f32[4096]{0:T(1024)S(1)} fusion(f32[4096]{0:T(1024)S(1)} %bitcast.48, s32[4096]{0:T(1024)S(1)} %broadcast_clamp_fusion.5), kind=kCustom, calls=%fused_computation.1.clone.1 | custom fusion | bytes 49152 | tf_op jit(solution)/shard_map/while/body/eval_jaxpr/gather | solution.py:241
  378.8 23.0 %gather_fusion = f32[4096]{0:T(1024)S(1)} fusion(f32[4096]{0:T(1024)S(1)} %bitcast.48, s32[4096]{0:T(1024)S(1)} %broadcast_clamp_fusion.5), kind=kCustom, calls=%fused_computation.1.clone.1 | custom fusion | bytes 49152 | tf_op jit(solution)/shard_map/while/body/eval_jaxpr/gather | solution.py:241
  403.9 5.0 collective-permute-start.1
  416.6 23.0 %gather_fusion = f32[4096]{0:T(1024)S(1)} fusion(f32[4096]{0:T(1024)S(1)} %bitcast.48, s32[4096]{0:T(1024)S(1)} %broadcast_clamp_fusion.5), kind=kCustom, calls=%fused_computation.1.clone.1 | custom fusion | bytes 49152 | tf_op jit(solution)/shard_map/while/body/eval_jaxpr/gather | solution.py:241
  441.7 5.0 collective-permute-start.1
  454.4 23.0 %gather_fusion = f32[4096]{0:T(1024)S(1)} fusion(f32[4096]{0:T(1024)S(1)} %bitcast.48, s32[4096]{0:T(1024)S(1)} %broadcast_clamp_fusion.5), kind=kCustom, calls=%fused_computation.1.clone.1 | custom fusion | bytes 49152 | tf_op jit(solution)/shard_map/while/body/eval_jaxpr/gather | solution.py:241
  486.6 6.2 collective-permute-start.3
  493.8 23.0 %gather_fusion = f32[4096]{0:T(1024)S(1)} fusion(f32[4096]{0:T(1024)S(1)} %bitcast.48, s32[4096]{0:T(1024)S(1)} %broadcast_clamp_fusion.5), kind=kCustom, calls=%fused_computation.1.clone.1 | custom fusion | bytes 49152 | tf_op jit(solution)/shard_map/while/body/eval_jaxpr/gather | solution.py:241
  526.0 6.7 collective-permute-start.3
  533.7 23.0 %gather_fusion = f32[4096]{0:T(1024)S(1)} fusion(f32[4096]{0:T(1024)S(1)} %bitcast.48, s32[4096]{0:T(1024)S(1)} %broadcast_clamp_fusion.5), kind=kCustom, calls=%fused_computation.1.clone.1 | custom fusion | bytes 49152 | tf_op jit(solution)/shard_map/while/body/eval_jaxpr/gather | solution.py:241
  565.9 6.7 collective-permute-start.3
  573.6 23.0 %gather_fusion = f32[4096]{0:T(1024)S(1)} fusion(f32[4096]{0:T(1024)S(1)} %bitcast.48, s32[4096]{0:T(1024)S(1)} %broadcast_clamp_fusion.5), kind=kCustom, calls=%fused_computation.1.clone.1 | custom fusion | bytes 49152 | tf_op jit(solution)/shard_map/while/body/eval_jaxpr/gather | solution.py:241
  605.8 6.7 collective-permute-start.3
  613.5 23.0 %gather_fusion = f32[4096]{0:T(1024)S(1)} fusion(f32[4096]{0:T(1024)S(1)} %bitcast.48, s32[4096]{0:T(1024)S(1)} %broadcast_clamp_fusion.5), kind=kCustom, calls=%fused_computation.1.clone.1 | custom fusion | bytes 49152 | tf_op jit(solution)/shard_map/while/body/eval_jaxpr/gather | solution.py:241
  645.7 6.7 collective-permute-start.3
  653.4 23.0 %gather_fusion = f32[4096]{0:T(1024)S(1)} fusion(f32[4096]{0:T(1024)S(1)} %bitcast.48, s32[4096]{0:T(1024)S(1)} %broadcast_clamp_fusion.5), kind=kCustom, calls=%fused_computation.1.clone.1 | custom fusion | bytes 49152 | tf_op jit(solution)/shard_map/while/body/eval_jaxpr/gather | solution.py:241
  685.6 6.7 collective-permute-start.3
  693.3 23.0 %gather_fusion = f32[4096]{0:T(1024)S(1)} fusion(f32[4096]{0:T(1024)S(1)} %bitcast.48, s32[4096]{0:T(1024)S(1)} %broadcast_clamp_fusion.5), kind=kCustom, calls=%fused_computation.1.clone.1 | custom fusion | bytes 49152 | tf_op jit(solution)/shard_map/while/body/eval_jaxpr/gather | solution.py:241
  725.5 6.7 collective-permute-start.3
  733.2 23.0 %gather_fusion = f32[4096]{0:T(1024)S(1)} fusion(f32[4096]{0:T(1024)S(1)} %bitcast.48, s32[4096]{0:T(1024)S(1)} %broadcast_clamp_fusion.5), kind=kCustom, calls=%fused_computation.1.clone.1 | custom fusion | bytes 49152 | tf_op jit(solution)/shard_map/while/body/eval_jaxpr/gather | solution.py:241
  757.2 18.7 %all-to-all-start.2 = ((f32[128,1,384]{2,1,0:T(1,128)}), f32[128,1,384]{2,1,0:T(1,128)S(1)}, u32[]{:S(2)}, u32[]{:S(2)}) async-start(f32[128,1,384]{2,1,0:T(1,128)} %copy.52), calls=%async_computation.2 | async-start | bytes 393216 | tf_op jit(solution)/shard_map/all_to_all | solution.py:249
  776.1 10.6 %all-to-all-done.2 = f32[128,1,384]{2,1,0:T(1,128)S(1)} async-done(((f32[128,1,384]{2,1,0:T(1,128)}), f32[128,1,384]{2,1,0:T(1,128)S(1)}, u32[]{:S(2)}, u32[]{:S(2)}) %all-to-all-start.2) | async-done | bytes 196640 | tf_op jit(solution)/shard_map/all_to_all | solution.py:249
  786.9 196.6 %gather_fusion.3 = f32[24576]{0:T(1024)S(1)} fusion(f32[128,12,32]{0,2,1:T(8,128)S(1)} %bitcast.47, s32[24576]{0:T(1024)S(1)} %reshape.352), kind=kCustom, calls=%fused_computation.3 | custom fusion | bytes 491520 | tf_op jit(solution)/shard_map/gather | solution.py:260
  (1243 shorter events, 198.8 us)
Async XLA Ops:
  179.0 76.5 %all-to-all-start.1 = ((s32[128,1,32]{2,1,0:T(1,128)}), s32[128,1,32]{2,1,0:T(1,128)S(1)}, u32[]{:S(2)}, u32[]{:S(2)}) async-start(s32[128,1,32]{2,1,0:T(1,128)} %copy.50), calls=%async_computation.1 | async-start | bytes 131072 | tf_op jit(solution)/shard_map/all_to_all | solution.py:187
  191.1 56.2 %collective-permute-start.6 = (f32[1,128]{1,0:T(1,128)}, f32[1,128]{1,0:T(1,128)}, u32[]{:S(2)}, u32[]{:S(2)}) collective-permute-start(f32[1,128]{1,0:T(1,128)} %get-tuple-element.1279), channel_id=1, source_target_pairs={{0,16},{16,32},{32,48},{48,64},{64,80},{80,96},{96,112},{1,17},{17... | collective-permute-start | bytes 1544 | tf_op jit(solution)/shard_map/ppermute | solution.py:27
  194.7 52.7 %collective-permute-start.7 = (f32[1,128]{1,0:T(1,128)}, f32[1,128]{1,0:T(1,128)}, u32[]{:S(2)}, u32[]{:S(2)}) collective-permute-start(f32[1,128]{1,0:T(1,128)} %get-tuple-element.1278), channel_id=1, source_target_pairs={{16,0},{32,16},{48,32},{64,48},{80,64},{96,80},{112,96},{17,1},{33... | collective-permute-start | bytes 1544 | tf_op jit(solution)/shard_map/ppermute | solution.py:28
  197.3 93.0 %collective-permute-start.5 = (f32[32,1]{1,0:T(8,128)}, f32[32,1]{1,0:T(8,128)S(1)}, u32[]{:S(2)}, u32[]{:S(2)}) collective-permute-start(f32[32,1]{1,0:T(8,128)} %slice.442), channel_id=1, source_target_pairs={{0,1},{1,2},{2,3},{3,4},{4,5},{5,6},{6,7},{7,8},{8,9},{9,10},{10,1... | collective-permute-start | bytes 392 | tf_op jit(solution)/shard_map/ppermute | solution.py:36
  200.9 53.2 %collective-permute-start.4 = (f32[1,128]{1,0:T(1,128)}, f32[1,128]{1,0:T(1,128)}, u32[]{:S(2)}, u32[]{:S(2)}) collective-permute-start(f32[1,128]{1,0:T(1,128)} %slice.441), channel_id=1, source_target_pairs={{0,16},{16,32},{32,48},{48,64},{64,80},{80,96},{96,112},{1,17},{17... | collective-permute-start | bytes 1544 | tf_op jit(solution)/shard_map/ppermute | solution.py:36
  248.1 6.6 collective-permute-start.8
  249.4 6.1 collective-permute-start.9
  255.5 21.7 %all-to-all-start = ((f32[128,1,384]{2,1,0:T(1,128)}), f32[128,1,384]{2,1,0:T(1,128)S(1)}, u32[]{:S(2)}, u32[]{:S(2)}) async-start(f32[128,1,384]{2,1,0:T(1,128)} %copy.46), calls=%async_computation | async-start | bytes 393216 | tf_op jit(solution)/shard_map/all_to_all | solution.py:180
  326.1 7.3 collective-permute-start
  334.1 5.9 collective-permute-start.2
  364.2 7.0 collective-permute-start
  366.1 5.7 collective-permute-start.1
  371.9 5.9 collective-permute-start.2
  402.0 7.0 collective-permute-start
  403.9 5.7 collective-permute-start.1
  409.7 5.9 collective-permute-start.2
  439.8 7.0 collective-permute-start
  441.7 5.7 collective-permute-start.1
  447.5 5.9 collective-permute-start.2
  477.6 7.0 collective-permute-start
  479.5 5.7 collective-permute-start.1
  485.3 7.5 collective-permute-start.2
  486.6 7.1 collective-permute-start.3
  517.0 7.0 collective-permute-start
  518.9 5.7 collective-permute-start.1
  524.7 8.0 collective-permute-start.2
  526.0 7.6 collective-permute-start.3
  556.9 7.0 collective-permute-start
  558.8 5.7 collective-permute-start.1
  564.6 8.0 collective-permute-start.2
  565.9 7.6 collective-permute-start.3
  596.8 7.0 collective-permute-start
  598.7 5.7 collective-permute-start.1
  604.5 8.0 collective-permute-start.2
  605.8 7.6 collective-permute-start.3
  636.7 7.0 collective-permute-start
  638.6 5.7 collective-permute-start.1
  644.4 8.0 collective-permute-start.2
  645.7 7.6 collective-permute-start.3
  676.6 7.0 collective-permute-start
  678.5 5.7 collective-permute-start.1
  684.3 8.0 collective-permute-start.2
  685.6 7.6 collective-permute-start.3
  716.5 7.0 collective-permute-start
  718.4 5.7 collective-permute-start.1
  724.2 8.0 collective-permute-start.2
  725.5 7.6 collective-permute-start.3
  757.2 29.5 %all-to-all-start.2 = ((f32[128,1,384]{2,1,0:T(1,128)}), f32[128,1,384]{2,1,0:T(1,128)S(1)}, u32[]{:S(2)}, u32[]{:S(2)}) async-start(f32[128,1,384]{2,1,0:T(1,128)} %copy.52), calls=%async_computation.2 | async-start | bytes 393216 | tf_op jit(solution)/shard_map/all_to_all | solution.py:249
  (28 other events, 2611.8 us)
where the time goes:
time: 986 us; the launch traced here: 984 us
  local copies, waits for them, and re-layouts  683 us (69%)
  starting transfers between devices  225 us (23%)
  waiting for transfers between devices  33.1 us (3%)
  other arithmetic  26.3 us (3%)
  matrix products  12.3 us (1%)
    gather x12, local copies, waits for them, and re-layouts, ocean_turn(): level_now.reshape(tile_rows * tile_cols)[flat_cells]  276 us
    gather x1, local copies, waits for them, and re-layouts, per_device(): returned[tile_grid, step_grid, slot_grid].reshape(blocks, STEPS * MPB)  197 us
    gather x12, local copies, waits for them, and re-layouts, per_device(): first_index = jnp.searchsorted(sorted_tiles, sorted_tiles, side='left')  141 us
    ppermute x26, starting transfers between devices, padded_2(): before = lax.ppermute(last, axis, up)  134 us
    ppermute x26, starting transfers between devices, padded_2(): after = lax.ppermute(leading, axis, down)  42.6 us
  transfers between devices with their start and end apart: 57, of which 26 were waited for; matrix products, arithmetic and copies ran while one was open for 7% of the time, Pallas kernels for 0%

commit v1 on v0

v1 whole, which is shorter than its diff:
```python
import jax
import jax.numpy as jnp
from jax import lax
from jax.experimental import pallas as pl
from jax.experimental.pallas import tpu as pltpu
from jax.sharding import PartitionSpec as P

RB = 128
MPB = 32
STEPS = 12
TX = 32
TY = 128
REACH = 16

gravity = 9.81
step_seconds = 300.0
cell_metres = 3000.0
river_manning = 0.035
ocean_manning = 0.025
depth_floor = 0.05
GT = gravity * step_seconds
POWER = -7.0 / 3.0

F32 = jnp.float32
BF16 = jnp.bfloat16
I32 = jnp.int32
MESH = pl.DeviceIdType.MESH
NT = (((1,), (1,)), ((), ()))

WIDTHS = [STEPS - 1 - k for k in range(STEPS)]
STARTS = [sum(WIDTHS[:k]) for k in range(STEPS)]
VM = pl.BlockSpec(memory_space=pltpu.VMEM)
ROWS, COLS = 56, 256


def struct(*shape, dtype=F32):
    return jax.ShapeDtypeStruct(shape, dtype)


def iota(shape, axis):
    return lax.broadcasted_iota(I32, shape, axis)


def split(value):
    high = value.astype(BF16).astype(F32)
    return high, value - high


def lanes(value, shift):
    shift = shift % value.shape[1]
    return value if shift == 0 else pltpu.roll(value, shift, axis=1)


def friction(unit_flow, face_depth, manning):
    floor = jnp.maximum(face_depth, depth_floor)
    return 1.0 + (GT * manning * manning) * jnp.abs(unit_flow) * jnp.exp(POWER * jnp.log(floor))


def to_dense16(value):
    return jnp.concatenate([value[16 * q : 16 * q + 16] for q in range(4)], axis=1)


def swap_groups(parts):
    lane = iota(parts[0].shape, 1) // 32
    done = []
    for p in range(4):
        total = lanes(parts[0], -32 * p)
        for q in range(1, 4):
            total = jnp.where(lane == q, lanes(parts[q], 32 * (q - p)), total)
        done.append(total)
    return done


def river_kernel(
    depth_ref, flow_ref, bed_ref, width_ref, length_ref, runoff_ref, into_ref, prev_ref, tile_ref, cell_ref,
    sea_ref, seabed_ref, wet_ref, east_ref, north_ref,
    depth_out, send_out, tile_out, slot_out, fields_out, left_out, right_out,
    masks, series,
):
    seabed = seabed_ref[...]
    level = jnp.where(wet_ref[...] == 1, jnp.maximum(sea_ref[...], seabed), seabed)
    fields = [level, seabed, east_ref[...], north_ref[...]]
    lane = iota((TX, TY), 1)
    left = fields[0]
    right = lanes(fields[0], 16)
    for i in range(4):
        fields_out[i] = fields[i]
        if i:
            left = jnp.where(lane // 16 == i, lanes(fields[i], 16 * i), left)
            right = jnp.where(lane // 16 == i, lanes(fields[i], 16 * i + 16), right)
    left_out[...] = left
    right_out[...] = right

    tile = to_dense16(jnp.transpose(tile_ref[:, 0, :]))
    cell = to_dense16(jnp.transpose(cell_ref[...]))
    tile_out[...] = tile
    upper = (iota((128, 256), 0) < iota((128, 256), 1)).astype(F32).astype(BF16)
    tiles_of = iota((128, 128), 0)
    carry = jnp.zeros((128, 128), F32)
    hits, ranks = [], []
    for a in range(16):
        hit = (tiles_of == tile[a : a + 1, :]).astype(F32)
        hits.append(hit.astype(BF16))
        counted = jnp.dot(hits[a], upper, preferred_element_type=F32)
        ranks.append(jnp.sum(hit * (counted[:, :128] + carry), axis=0, keepdims=True))
        carry = carry + counted[:, 128:]
    slot = jnp.concatenate(ranks, axis=0).astype(I32)
    slot_out[...] = slot

    bed, width, into = bed_ref[...], width_ref[...], into_ref[...]
    lane = iota((64, RB), 1)
    inland = lane < RB - MPB
    index = jnp.minimum(into, RB - 1)
    below_bed = jnp.where(inland, jnp.take_along_axis(bed, index, axis=1, mode="promise_in_bounds"), bed)
    previous = jnp.concatenate([jnp.zeros((64, RB - MPB), F32), jnp.transpose(prev_ref[...])], axis=1)
    for offset in range(1, REACH + 1):
        masks[offset - 1] = (pltpu.roll(into, offset, axis=1) == lane).astype(F32)
    face_bed = jnp.maximum(bed, below_bed)
    pull = GT / length_ref[...]
    rate = step_seconds / (width * length_ref[...])
    runoff = runoff_ref[...]

    def turn(step, carry):
        depth, flow = carry
        surface = bed + depth
        below = jnp.where(inland, jnp.take_along_axis(surface, index, axis=1, mode="promise_in_bounds"), previous)
        face = jnp.maximum(surface, below) - face_bed
        drive = pull * jnp.maximum(face, 0.0) * (surface - below)
        flow = (flow + drive) / friction(flow, face, river_manning)
        discharge = flow * width
        inflow = runoff - discharge
        for offset in range(1, REACH + 1):
            inflow = inflow + masks[offset - 1] * pltpu.roll(discharge, offset, axis=1)
        series[step] = to_dense16(discharge[:, RB - MPB :])
        return depth + rate * inflow, flow

    depth, _ = lax.fori_loop(0, STEPS, turn, (depth_ref[...], flow_ref[...]))
    depth_out[...] = depth

    cells = cell.astype(F32)
    slots_of = iota((32, 128), 0)
    total = jnp.zeros((128, 512), F32)
    for a in range(16):
        mine = slots_of == slot[a : a + 1, :]
        pieces = []
        for k in range(STEPS + 1):
            row = series[k, a : a + 1, :] if k < STEPS else cells[a : a + 1, :]
            pieces.append(
                jnp.concatenate(
                    [jnp.where(mine, part, 0.0).astype(BF16) for part in split(row)], axis=1
                )
            )
        weights = jnp.concatenate(pieces + [pieces[-1]] * 3, axis=0)
        both = jnp.concatenate([hits[a], hits[a]], axis=1)
        total = total + lax.dot_general(both, weights, NT, preferred_element_type=F32)
    for j in range(4):
        send_out[:, j, :] = total[:, 128 * j : 128 * j + 128]


def source_kernel(recv_ref, src_out, left_out, right_out, row_out, col_out):
    lane = iota((32, 128), 1)
    dense = []
    for j in range(3):
        dense += swap_groups([recv_ref[32 * q : 32 * q + 32, j, :] for q in range(4)])
    cell = recv_ref[0:32, 3, :]
    for q in range(1, 4):
        cell = jnp.where(lane // 32 == q, recv_ref[32 * q : 32 * q + 32, 3, :], cell)
    cell = cell.astype(I32)
    row, col = cell // TY, cell % TY
    row_out[...] = row
    col_out[...] = col
    halves = [split(value) for value in dense]
    rows_of, cols_of = iota((TX, 128), 0), iota((TY, 128), 0)
    total = jnp.zeros((STEPS * TX, TY), F32)
    for a in range(32):
        mine = rows_of == row[a : a + 1, :]
        there = (cols_of == col[a : a + 1, :]).astype(F32).astype(BF16)
        pieces = [
            jnp.concatenate([jnp.where(mine, part[a : a + 1, :], 0.0).astype(BF16) for part in pair], axis=1)
            for pair in halves
        ]
        total = total + lax.dot_general(
            jnp.concatenate(pieces, axis=0), jnp.concatenate([there, there], axis=1), NT, preferred_element_type=F32
        )
    left = right = jnp.zeros((TX, TY), F32)
    for k in range(STEPS):
        now = total[TX * k : TX * k + TX] * (step_seconds / (cell_metres * cell_metres))
        src_out[k] = now
        if WIDTHS[k]:
            here = (lane >= STARTS[k]) & (lane < STARTS[k] + WIDTHS[k])
            left = jnp.where(here, lanes(now, STARTS[k]), left)
            right = jnp.where(here, lanes(now, STARTS[k] - (TY - WIDTHS[k])), right)
    left_out[...] = left
    right_out[...] = right


def stack_rows(own, low, up):
    upper_half = iota((8, own.shape[1]), 0) >= 4
    return jnp.concatenate(
        [own, low[0:8], jnp.where(upper_half, up[0:8], low[8:16]), up[8:16]], axis=0
    )


def ocean_kernel(
    fields_ref, flow_ref, fup_ref, fpr_ref, fpl_ref, fcor_ref,
    src_ref, slow_ref, sup_ref, spr_ref, spl_ref, scor_ref, row_ref, col_ref,
    level_out, reply_out, levels,
):
    river, coast = lax.axis_index("river"), lax.axis_index("coast")
    rivers, coasts = lax.axis_size("river"), lax.axis_size("coast")
    line = iota((ROWS, COLS), 0)
    place = iota((ROWS, COLS), 1)
    line_ok = (line < 32) | ((line < 44) & (river < rivers - 1)) | ((line >= 44) & (river > 0))
    place_ok = (place < 128) | ((place < 192) & (coast < coasts - 1)) | ((place >= 192) & (coast > 0))
    inside = line_ok & place_ok
    half = iota((ROWS, TY), 1) < 64

    from_right = stack_rows(fpr_ref[...], fcor_ref[0], fcor_ref[1])
    from_left = stack_rows(fpl_ref[...], fcor_ref[2], fcor_ref[3])
    state = []
    for i in range(4):
        own = stack_rows(fields_ref[i], flow_ref[i], fup_ref[i])
        side = jnp.where(half, lanes(from_right, -16 * i), lanes(from_left, 112 - 16 * i))
        state.append(jnp.where(inside, jnp.concatenate([own, side], axis=1), 0.0))
    level, bed, east, north = state
    bed_east = jnp.maximum(bed, pltpu.roll(bed, ROWS - 1, axis=0))
    bed_north = jnp.maximum(bed, pltpu.roll(bed, COLS - 1, axis=1))
    next_right = stack_rows(spr_ref[...], scor_ref[0], scor_ref[1])
    next_left = stack_rows(spl_ref[...], scor_ref[2], scor_ref[3])

    def inertial(unit_flow, upper, lower, bed_face):
        face = jnp.maximum(upper, lower) - bed_face
        drive = (GT / cell_metres) * jnp.maximum(face, 0.0) * (upper - lower)
        return (unit_flow + drive) / friction(unit_flow, face, ocean_manning)

    for k in range(STEPS):
        east = inertial(east, level, pltpu.roll(level, ROWS - 1, axis=0), bed_east)
        north = inertial(north, level, pltpu.roll(level, COLS - 1, axis=1), bed_north)
        own = stack_rows(src_ref[k], slow_ref[k], sup_ref[k])
        side = jnp.where(
            half, lanes(next_right, -STARTS[k]), lanes(next_left, TY - WIDTHS[k] - STARTS[k])
        )
        source = jnp.concatenate([own, side], axis=1)
        spread = east - pltpu.roll(east, 1, axis=0) + north - pltpu.roll(north, 1, axis=1)
        level = jnp.where(inside, level - (step_seconds / cell_metres) * spread + source, 0.0)
        levels[TX * k : TX * k + TX, :] = level[0:TX, 0:TY]
    level_out[...] = level[0:TX, 0:TY]

    high, low = split(levels[...])
    table = jnp.concatenate([high.astype(BF16), low.astype(BF16)], axis=1)
    rows_of, cols_of = iota((TX, 128), 0), iota((TY, 128), 0)
    picked = [[] for _ in range(STEPS)]
    for a in range(32):
        there = (cols_of == col_ref[a : a + 1, :]).astype(F32).astype(BF16)
        found = jnp.dot(table, jnp.concatenate([there, there], axis=0), preferred_element_type=F32)
        mine = rows_of == row_ref[a : a + 1, :]
        for k in range(STEPS):
            picked[k].append(jnp.sum(jnp.where(mine, found[TX * k : TX * k + TX], 0.0), axis=0, keepdims=True))
    for j in range(3):
        parts = swap_groups([jnp.concatenate(picked[4 * j + p], axis=0) for p in range(4)])
        for q in range(4):
            reply_out[32 * q : 32 * q + 32, j, :] = parts[q]
    reply_out[:, 3, :] = jnp.zeros((128, 128), F32)


def mouth_kernel(ret_ref, tile_ref, slot_ref, out_ref):
    table = jnp.concatenate([jnp.transpose(ret_ref[:, j, :]) for j in range(3)], axis=0)
    high, low = split(table)
    table = jnp.concatenate([high.astype(BF16), low.astype(BF16)], axis=1)
    tiles_of, slots_of = iota((128, 128), 0), iota((32, 128), 0)
    picked = [[] for _ in range(STEPS)]
    for a in range(16):
        hit = (tiles_of == tile_ref[a : a + 1, :]).astype(F32).astype(BF16)
        found = jnp.dot(table, jnp.concatenate([hit, hit], axis=0), preferred_element_type=F32)
        mine = slots_of == slot_ref[a : a + 1, :]
        for k in range(STEPS):
            picked[k].append(jnp.sum(jnp.where(mine, found[32 * k : 32 * k + 32], 0.0), axis=0, keepdims=True))
    for j in range(3):
        parts = swap_groups([jnp.concatenate(picked[4 * j + p], axis=0) for p in range(4)])
        for q in range(4):
            out_ref[16 * q : 16 * q + 16, 128 * j : 128 * j + 128] = parts[q]


def around():
    river, coast = lax.axis_index("river"), lax.axis_index("coast")
    rivers, coasts = lax.axis_size("river"), lax.axis_size("coast")
    return river, coast, rivers, coasts


def greet(devices):
    barrier = pltpu.get_barrier_semaphore()
    for device in devices:
        pl.semaphore_signal(barrier, inc=1, device_id=device, device_id_type=MESH)
    pl.semaphore_wait(barrier, len(devices))


def ring_devices():
    river, coast, rivers, coasts = around()
    return [((river + d) % rivers, coast) for d in range(1, rivers)] + [
        (river, (coast + d) % coasts) for d in range(1, coasts)
    ]


def beside_devices(corners_only):
    river, coast, rivers, coasts = around()
    devices = [((river + r) % rivers, (coast + c) % coasts) for r in (-1, 1) for c in (-1, 1)]
    if not corners_only:
        devices += [((river + r) % rivers, coast) for r in (-1, 1)]
        devices += [(river, (coast + c) % coasts) for c in (-1, 1)]
    return devices


def remote(src, dst, send, recv, index, device):
    return pltpu.make_async_remote_copy(
        src_ref=src, dst_ref=dst, send_sem=send.at[index], recv_sem=recv.at[index], device_id=device,
        device_id_type=MESH,
    )


def over_river(src, dst, send, recv, local):
    river, coast, rivers, _ = around()
    copies = [
        remote(src.at[(river + d) % rivers], dst.at[river], send, recv, d - 1, ((river + d) % rivers, coast))
        for d in range(1, rivers)
    ]
    return copies, pltpu.make_async_copy(src.at[river], dst.at[river], local)


def over_coast(src, dst, send, recv, local):
    river, coast, _, coasts = around()
    copies = [
        remote(
            src.at[:, (coast + d) % coasts], dst.at[:, coast], send, recv, d - 1, (river, (coast + d) % coasts)
        )
        for d in range(1, coasts)
    ]
    return copies, pltpu.make_async_copy(src.at[:, coast], dst.at[:, coast], local)


def run(copies, local):
    for copy in copies:
        copy.start()
    local.start()
    for copy in copies:
        copy.wait()
    local.wait()


def corner_copies(left, right, corners, send, recv, first):
    river, coast, rivers, coasts = around()
    before, after = (river - 1) % rivers, (river + 1) % rivers
    west, east = (coast - 1) % coasts, (coast + 1) % coasts
    return [
        remote(left.at[0:16], corners.at[0], send, recv, first, (before, west)),
        remote(left.at[16:32], corners.at[1], send, recv, first + 1, (after, west)),
        remote(right.at[0:16], corners.at[2], send, recv, first + 2, (before, east)),
        remote(right.at[16:32], corners.at[3], send, recv, first + 3, (after, east)),
    ]


def side_copies(left, right, from_right, from_left, send, recv, first):
    river, coast, _, coasts = around()
    return [
        remote(left, from_right, send, recv, first, (river, (coast - 1) % coasts)),
        remote(right, from_left, send, recv, first + 1, (river, (coast + 1) % coasts)),
    ]


def row_copies(whole, low, up, send, recv, first):
    river, coast, rivers, _ = around()
    return [
        remote(whole.at[:, 0:16], low, send, recv, first, ((river - 1) % rivers, coast)),
        remote(whole.at[:, 16:32], up, send, recv, first + 1, ((river + 1) % rivers, coast)),
    ]


def outward_kernel(
    send_ref, fields, left, right, recv_out, low, up, from_right, from_left, corners,
    middle, send_r, recv_r, send_c, recv_c, send_h, recv_h, local,
):
    greet(ring_devices() + beside_devices(True))
    copies, own = over_river(send_ref, middle, send_r, recv_r, local.at[0])
    halo = (
        side_copies(left, right, from_right, from_left, send_h, recv_h, 0)
        + row_copies(fields, low, up, send_h, recv_h, 2)
        + corner_copies(left, right, corners, send_h, recv_h, 4)
    )
    run(copies, own)
    for copy in halo:
        copy.start()
    run(*over_coast(middle, recv_out, send_c, recv_c, local.at[1]))
    for copy in halo:
        copy.wait()


def beside_kernel(whole, left, right, low, up, from_right, from_left, corners, send_h, recv_h):
    greet(beside_devices(False))
    halo = (
        side_copies(left, right, from_right, from_left, send_h, recv_h, 0)
        + row_copies(whole, low, up, send_h, recv_h, 2)
        + corner_copies(left, right, corners, send_h, recv_h, 4)
    )
    for copy in halo:
        copy.start()
    for copy in halo:
        copy.wait()


def back_kernel(reply, out, middle, send_r, recv_r, send_c, recv_c, local):
    greet(ring_devices())
    run(*over_coast(reply, middle, send_c, recv_c, local.at[0]))
    run(*over_river(middle, out, send_r, recv_r, local.at[1]))


def call(kernel, outs, scratch=(), remote_id=None):
    params = (
        pltpu.CompilerParams(vmem_limit_bytes=48 * 2**20)
        if remote_id is None
        else pltpu.CompilerParams(vmem_limit_bytes=48 * 2**20, collective_id=remote_id, has_side_effects=True)
    )

    def apply(*args):
        return pl.pallas_call(
            kernel,
            out_shape=outs,
            in_specs=[VM] * len(args),
            out_specs=jax.tree.map(lambda _: VM, outs),
            scratch_shapes=list(scratch),
            compiler_params=params,
        )(*args)

    return apply


def per_device(
    reach_depth, reach_flow, reach_bed, reach_width, reach_length, runoff, flows_into, mouth_prev, mouth_tile,
    mouth_cell, sea_level, sea_bed, wet_mask, flux_east, flux_north,
):
    rivers, coasts = lax.axis_size("river"), lax.axis_size("coast")
    dma = pltpu.SemaphoreType.DMA
    depth_after, send, tile, slot, fields, left, right = call(
        river_kernel,
        (
            struct(64, 128), struct(128, 4, 128), struct(16, 128, dtype=I32), struct(16, 128, dtype=I32),
            struct(4, 32, 128), struct(32, 128), struct(32, 128),
        ),
        (pltpu.VMEM((REACH, 64, 128), F32), pltpu.VMEM((STEPS, 16, 128), F32)),
    )(
        reach_depth, reach_flow, reach_bed, reach_width, reach_length, runoff, flows_into,
        mouth_prev.T, jnp.transpose(mouth_tile, (1, 2, 0)), mouth_cell.T,
        sea_level, sea_bed, wet_mask, flux_east, flux_north,
    )
    halo = (struct(32, 128), struct(32, 128), struct(4, 16, 128))
    recv, *field_halo = call(
        outward_kernel,
        (struct(rivers, coasts, 4, 128), struct(4, 16, 128), struct(4, 16, 128)) + halo,
        (
            pltpu.VMEM((rivers, coasts, 4, 128), F32),
            dma((rivers - 1,)), dma((rivers - 1,)), dma((coasts - 1,)), dma((coasts - 1,)), dma((8,)), dma((8,)),
            dma((2,)),
        ),
        0,
    )(send.reshape(rivers, coasts, 4, 128), fields, left, right)
    sources, left, right, row, col = call(
        source_kernel,
        (
            struct(STEPS, 32, 128), struct(32, 128), struct(32, 128), struct(32, 128, dtype=I32),
            struct(32, 128, dtype=I32),
        ),
    )(recv.reshape(128, 4, 128))
    source_halo = call(
        beside_kernel,
        (struct(STEPS, 16, 128), struct(STEPS, 16, 128)) + halo,
        (dma((8,)), dma((8,))),
        1,
    )(sources, left, right)
    level_after, reply = call(
        ocean_kernel,
        (struct(32, 128), struct(128, 4, 128)),
        (pltpu.VMEM((STEPS * TX, TY), F32),),
    )(fields, *field_halo, sources, *source_halo, row, col)
    returned = call(
        back_kernel,
        struct(rivers, coasts, 4, 128),
        (
            pltpu.VMEM((rivers, coasts, 4, 128), F32),
            dma((rivers - 1,)), dma((rivers - 1,)), dma((coasts - 1,)), dma((coasts - 1,)), dma((2,)),
        ),
        2,
    )(reply.reshape(rivers, coasts, 4, 128))
    mouth_level = call(mouth_kernel, struct(64, 384))(returned.reshape(128, 4, 128), tile, slot)
    return depth_after, level_after, mouth_level


def solution(mesh):
    both = P(("river", "coast"), None)
    grid = P("river", "coast")
    placed = (both,) * 8 + (P(("river", "coast"), None, None), both) + (grid,) * 5
    return jax.shard_map(
        per_device, mesh=mesh, in_specs=placed, out_specs=(both, grid, both), check_vma=False
    )
```

time: 986 us -> 70.5 us (0.07)
  local copies, waits for them, and re-layouts: 683 us -> 11 us
  starting transfers between devices: 225 us -> 0 us
  Pallas kernels: 0 us -> 57.7 us
  waiting for transfers between devices: 33.1 us -> 0 us
  other arithmetic: 26.3 us -> 0 us
  matrix products: 12.3 us -> 0 us
    gather x26 -> x0, local copies, waits for them, and re-layouts: 626 us -> none  [the longest x12 276 us: ocean_turn(): level_now.reshape(tile_rows * tile_cols)[flat_cells]]
    ppermute x54 -> x0, starting transfers between devices: 184 us -> none  [the longest x26 134 us: padded_2(): before = lax.ppermute(last, axis, up)]
    pallas_call x0 -> x7, Pallas kernels: none -> 57.7 us  [apply(): pl.pallas_call(kernel, out_shape=outs, in_specs=[VM] * len(args), out_spe...]
    all_to_all x3 -> x0, starting transfers between devices: 41 us -> none  [the longest x1 18.7 us: per_device(): lax.all_to_all(replies.reshape(devices, STEPS * capacity), ('river', 'coa...]
    all_to_all x3 -> x0, waiting for transfers between devices: 17 us -> none  [the longest x1 10.6 us: per_device(): lax.all_to_all(replies.reshape(devices, STEPS * capacity), ('river', 'coa...]
    ppermute x54 -> x0, waiting for transfers between devices: 16.1 us -> none  [the longest x26 16 us: padded_2(): before = lax.ppermute(last, axis, up)]
    dot_general x1 -> x0, matrix products: 12.3 us -> none  [per_device(): jnp.einsum('mr,kmc->krc', row_hits, weighted, precision=lax.Precision.HIG...]
    concatenate x290 -> x0, local copies, waits for them, and re-layouts: 11.6 us -> none  [the longest x276 10.9 us: gather_inflow(): jnp.concatenate([jnp.zeros((blocks, offset), jnp.float32), moved, jnp.zer...]
  transfers between devices with their start and end apart: 57 -> 0, of which waited for: 26 -> 0; matrix products, arithmetic and copies ran while one was open for 7% -> 0% of each run, Pallas kernels for 0% -> 0%
where the time goes in v1:
time: 70.5 us; the launch traced here: 69.4 us
  Pallas kernels  57.7 us (82%)
  local copies, waits for them, and re-layouts  11 us (16%)
  between operations  0.71 us (1%)
    pallas_call x7, Pallas kernels, apply(): pl.pallas_call(kernel, out_shape=outs, in_specs=[VM] * len(args), out_spe...  57.7 us
    unnamed x30, local copies, waits for them, and re-layouts  11 us

profile of v1, /device:TPU:1, one launch (start us, length us, event | category | flops | bytes accessed | tf_op | source)
XLA Modules:
  0.0 69.4 jit_solution(6392192820894936573)
XLA Ops:
  0.6 0.0 copy-start
  0.6 0.7 %copy-done = f32[64,128]{1,0:T(8,128)S(1)} copy-done((f32[64,128]{1,0:T(8,128)S(1)}, f32[64,128]{1,0:T(8,128)}, u32[]{:S(2)}) %copy-start) | copy-done | bytes 32792
  1.4 0.0 copy-start.1
  1.4 0.8 %copy-done.1 = f32[64,128]{1,0:T(8,128)S(1)} copy-done((f32[64,128]{1,0:T(8,128)S(1)}, f32[64,128]{1,0:T(8,128)}, u32[]{:S(2)}) %copy-start.1) | copy-done | bytes 32792
  2.2 0.0 copy-start.2
  2.2 0.8 %copy-done.2 = f32[64,128]{1,0:T(8,128)S(1)} copy-done((f32[64,128]{1,0:T(8,128)S(1)}, f32[64,128]{1,0:T(8,128)}, u32[]{:S(2)}) %copy-start.2) | copy-done | bytes 32792
  2.9 0.0 copy-start.3
  2.9 0.8 %copy-done.3 = f32[64,128]{1,0:T(8,128)S(1)} copy-done((f32[64,128]{1,0:T(8,128)S(1)}, f32[64,128]{1,0:T(8,128)}, u32[]{:S(2)}) %copy-start.3) | copy-done | bytes 32792
  3.7 0.0 copy-start.4
  3.7 0.8 %copy-done.4 = f32[64,128]{1,0:T(8,128)S(1)} copy-done((f32[64,128]{1,0:T(8,128)S(1)}, f32[64,128]{1,0:T(8,128)}, u32[]{:S(2)}) %copy-start.4) | copy-done | bytes 32792
  4.4 0.0 copy-start.5
  4.4 0.8 %copy-done.5 = f32[64,128]{1,0:T(8,128)S(1)} copy-done((f32[64,128]{1,0:T(8,128)S(1)}, f32[64,128]{1,0:T(8,128)}, u32[]{:S(2)}) %copy-start.5) | copy-done | bytes 32792
  5.2 0.0 copy-start.6
  5.2 0.8 %copy-done.6 = s32[64,128]{1,0:T(8,128)S(1)} copy-done((s32[64,128]{1,0:T(8,128)S(1)}, s32[64,128]{1,0:T(8,128)}, u32[]{:S(2)}) %copy-start.6) | copy-done | bytes 32792
  5.9 0.0 copy-start.7
  5.9 0.7 %copy-done.7 = f32[64,32]{0,1:T(8,128)S(1)} copy-done((f32[64,32]{0,1:T(8,128)S(1)}, f32[64,32]{0,1:T(8,128)}, u32[]{:S(2)}) %copy-start.7) | copy-done | bytes 8216
  6.7 0.0 copy-start.8
  6.7 0.7 %copy-done.8 = s32[64,32,1]{0,2,1:T(1,128)S(1)} copy-done((s32[64,32,1]{0,2,1:T(1,128)S(1)}, s32[64,32,1]{0,2,1:T(1,128)}, u32[]{:S(2)}) %copy-start.8) | copy-done | bytes 8216
  7.4 0.0 copy-start.9
  7.4 0.7 %copy-done.9 = s32[64,32]{0,1:T(8,128)S(1)} copy-done((s32[64,32]{0,1:T(8,128)S(1)}, s32[64,32]{0,1:T(8,128)}, u32[]{:S(2)}) %copy-start.9) | copy-done | bytes 8216
  8.1 0.0 copy-start.10
  8.1 0.7 %copy-done.10 = f32[32,128]{1,0:T(8,128)S(1)} copy-done((f32[32,128]{1,0:T(8,128)S(1)}, f32[32,128]{1,0:T(8,128)}, u32[]{:S(2)}) %copy-start.10) | copy-done | bytes 16408
  8.8 0.0 copy-start.11
  8.8 0.7 %copy-done.11 = f32[32,128]{1,0:T(8,128)S(1)} copy-done((f32[32,128]{1,0:T(8,128)S(1)}, f32[32,128]{1,0:T(8,128)}, u32[]{:S(2)}) %copy-start.11) | copy-done | bytes 16408
  9.5 0.0 copy-start.12
  9.5 0.7 %copy-done.12 = s32[32,128]{1,0:T(8,128)S(1)} copy-done((s32[32,128]{1,0:T(8,128)S(1)}, s32[32,128]{1,0:T(8,128)}, u32[]{:S(2)}) %copy-start.12) | copy-done | bytes 16408
  10.3 0.0 copy-start.13
  10.3 0.7 %copy-done.13 = f32[32,128]{1,0:T(8,128)S(1)} copy-done((f32[32,128]{1,0:T(8,128)S(1)}, f32[32,128]{1,0:T(8,128)}, u32[]{:S(2)}) %copy-start.13) | copy-done | bytes 16408
  11.0 0.0 copy-start.14
  11.0 0.7 %copy-done.14 = f32[32,128]{1,0:T(8,128)S(1)} copy-done((f32[32,128]{1,0:T(8,128)S(1)}, f32[32,128]{1,0:T(8,128)}, u32[]{:S(2)}) %copy-start.14) | copy-done | bytes 16408
  11.7 6.1 %shard_map.166 = (f32[64,128]{1,0:T(8,128)}, f32[128,4,128]{2,1,0:T(4,128)S(1)}, s32[16,128]{1,0:T(8,128)S(1)}, s32[16,128]{1,0:T(8,128)S(1)}, f32[4,32,128]{2,1...) custom-call(f32[64,128]{1,0:T(8,128)S(1)} %copy-done, f32[64,128]{1,0:T(8,128)S(1)} %copy-done.1, ...), custom_call_target="tpu_custom_call" | custom-call | tf_op jit(solution)/shard_map/pallas_call | solution.py:423
  17.8 19.9 %shard_map.167 = (f32[8,16,4,128]{3,2,1,0:T(4,128)S(1)}, f32[4,16,128]{2,1,0:T(8,128)S(1)}, f32[4,16,128]{2,1,0:T(8,128)S(1)}, f32[32,128]{1,0:T(8,128)S(1)}, f3...) custom-call(f32[8,16,4,128]{3,2,1,0:T(4,128)S(1)} %bitcast.10, f32[4,32,128]{2,1,0:T(8,128)S(1)} %get-tuple-element.29.fields.fields_ref, ...), custom_call_target="tpu_custom_call" | custom-call | tf_op jit(solution)/shard_map/pallas_call | solution.py:423
  37.7 2.0 %shard_map.168 = (f32[12,32,128]{2,1,0:T(8,128)S(1)}, f32[32,128]{1,0:T(8,128)S(1)}, f32[32,128]{1,0:T(8,128)S(1)}, s32[32,128]{1,0:T(8,128)S(1)}, s32[32,128]{1,0:T(8,128)S(1)}) custom-call(f32[128,4,128]{2,1,0:T(4,128)S(1)} %bitcast.9), custom_call_target="tpu_custom_call" | custom-call | tf_op jit(solution)/shard_map/pallas_call | solution.py:423
  39.7 9.3 %shard_map.169 = (f32[12,16,128]{2,1,0:T(8,128)S(1)}, f32[12,16,128]{2,1,0:T(8,128)S(1)}, f32[32,128]{1,0:T(8,128)S(1)}, f32[32,128]{1,0:T(8,128)S(1)}, f32[4,16,128]{2,1,0:T(8,128)S(1)}) custom-call(f32[12,32,128]{2,1,0:T(8,128)S(1)} %get-tuple-element.39.whole.src_ref, f32[32,128]{1,0:T(8,128)S(1)} %get-tuple-element.40.left, ...), custom_call_target="tpu_custom_call" | custom-call | tf_op jit(solution)/shard_map/pallas_call | solution.py:423
  48.9 4.1 %shard_map.170 = (f32[32,128]{1,0:T(8,128)}, f32[128,4,128]{2,1,0:T(4,128)S(1)}) custom-call(f32[4,32,128]{2,1,0:T(8,128)S(1)} %get-tuple-element.29.fields.fields_ref, f32[4,16,128]{2,1,0:T(8,128)S(1)} %get-tuple-element.33.flow_ref, f32[4,16,128]{2,1,0:T(8,128)S(1)} %get-tuple-element.34.fup_ref, f32[32,128]{1,0:T(8,128)S(1)} %get-tuple-element.35.fpr_ref, ...), custom_call_target="tpu_custom_call" | custom-call | tf_op jit(solution)/shard_map/pallas_call | solution.py:423
  53.1 14.5 %shard_map.171 = f32[8,16,4,128]{3,2,1,0:T(4,128)S(1)} custom-call(f32[8,16,4,128]{3,2,1,0:T(4,128)S(1)} %bitcast.8), custom_call_target="tpu_custom_call" | custom-call | tf_op jit(solution)/shard_map/pallas_call | solution.py:423
  67.6 1.8 %shard_map.172 = f32[64,384]{1,0:T(8,128)} custom-call(f32[128,4,128]{2,1,0:T(4,128)S(1)} %bitcast.7, s32[16,128]{1,0:T(8,128)S(1)} %get-tuple-element.51.tile_ref, s32[16,128]{1,0:T(8,128)S(1)} %get-tuple-element.52.slot_ref), custom_call_target="tpu_custom_call" | custom-call | tf_op jit(solution)/shard_map/pallas_call | solution.py:423
Async XLA Ops:
  0.6 0.8 %copy-start = (f32[64,128]{1,0:T(8,128)S(1)}, f32[64,128]{1,0:T(8,128)}, u32[]{:S(2)}) copy-start(f32[64,128]{1,0:T(8,128)} %depth_ref.1) | copy-start | bytes 98308
  1.4 0.8 %copy-start.1 = (f32[64,128]{1,0:T(8,128)S(1)}, f32[64,128]{1,0:T(8,128)}, u32[]{:S(2)}) copy-start(f32[64,128]{1,0:T(8,128)} %flow_ref.1) | copy-start | bytes 98308
  2.2 0.8 %copy-start.2 = (f32[64,128]{1,0:T(8,128)S(1)}, f32[64,128]{1,0:T(8,128)}, u32[]{:S(2)}) copy-start(f32[64,128]{1,0:T(8,128)} %bed_ref.1) | copy-start | bytes 98308
  2.9 0.8 %copy-start.3 = (f32[64,128]{1,0:T(8,128)S(1)}, f32[64,128]{1,0:T(8,128)}, u32[]{:S(2)}) copy-start(f32[64,128]{1,0:T(8,128)} %width_ref.1) | copy-start | bytes 98308
  3.7 0.8 %copy-start.4 = (f32[64,128]{1,0:T(8,128)S(1)}, f32[64,128]{1,0:T(8,128)}, u32[]{:S(2)}) copy-start(f32[64,128]{1,0:T(8,128)} %length_ref.1) | copy-start | bytes 98308
  4.4 0.8 %copy-start.5 = (f32[64,128]{1,0:T(8,128)S(1)}, f32[64,128]{1,0:T(8,128)}, u32[]{:S(2)}) copy-start(f32[64,128]{1,0:T(8,128)} %runoff_ref.1) | copy-start | bytes 98308
  5.2 0.8 %copy-start.6 = (s32[64,128]{1,0:T(8,128)S(1)}, s32[64,128]{1,0:T(8,128)}, u32[]{:S(2)}) copy-start(s32[64,128]{1,0:T(8,128)} %into_ref.1) | copy-start | bytes 98308
  5.9 0.7 %copy-start.7 = (f32[64,32]{0,1:T(8,128)S(1)}, f32[64,32]{0,1:T(8,128)}, u32[]{:S(2)}) copy-start(f32[64,32]{0,1:T(8,128)} %param.22) | copy-start | bytes 24580
  6.7 0.7 %copy-start.8 = (s32[64,32,1]{0,2,1:T(1,128)S(1)}, s32[64,32,1]{0,2,1:T(1,128)}, u32[]{:S(2)}) copy-start(s32[64,32,1]{0,2,1:T(1,128)} %param.23) | copy-start | bytes 24580
  7.4 0.7 %copy-start.9 = (s32[64,32]{0,1:T(8,128)S(1)}, s32[64,32]{0,1:T(8,128)}, u32[]{:S(2)}) copy-start(s32[64,32]{0,1:T(8,128)} %param.24) | copy-start | bytes 24580
  8.1 0.7 %copy-start.10 = (f32[32,128]{1,0:T(8,128)S(1)}, f32[32,128]{1,0:T(8,128)}, u32[]{:S(2)}) copy-start(f32[32,128]{1,0:T(8,128)} %sea_ref.1) | copy-start | bytes 49156
  8.8 0.7 %copy-start.11 = (f32[32,128]{1,0:T(8,128)S(1)}, f32[32,128]{1,0:T(8,128)}, u32[]{:S(2)}) copy-start(f32[32,128]{1,0:T(8,128)} %seabed_ref.1) | copy-start | bytes 49156
  9.5 0.7 %copy-start.12 = (s32[32,128]{1,0:T(8,128)S(1)}, s32[32,128]{1,0:T(8,128)}, u32[]{:S(2)}) copy-start(s32[32,128]{1,0:T(8,128)} %wet_ref.1) | copy-start | bytes 49156
  10.3 0.7 %copy-start.13 = (f32[32,128]{1,0:T(8,128)S(1)}, f32[32,128]{1,0:T(8,128)}, u32[]{:S(2)}) copy-start(f32[32,128]{1,0:T(8,128)} %east_ref.1) | copy-start | bytes 49156
  11.0 0.7 %copy-start.14 = (f32[32,128]{1,0:T(8,128)S(1)}, f32[32,128]{1,0:T(8,128)}, u32[]{:S(2)}) copy-start(f32[32,128]{1,0:T(8,128)} %north_ref.1) | copy-start | bytes 49156
